TPU v7x, 256 devices: a whole 4x4x8 slice. The times are simulated.
256 devices in a mesh: pair: 4 (over x), row: 64 (over z, y, core).
Axes of the slice: x: 4, y: 4, z: 8, core: 2. Of those that a mesh axis runs over, the one named last changes fastest.
Arguments:
- matrix: float32 [16384, 4096], P('row', 'pair'), may hold values from -18 to 18, as said below
- plan: int32 [2, 8], replicated, may hold values from 0 to 7, each once within a row
Outputs:
- rotated: float32 [16384, 4096], P('row', 'pair')
Inputs may be any that keep to these rules, and one draw needn't show every extreme that they name: `matrix`: an entry's magnitude is at most 18. `plan`: each row names every block number once.
All inputs are finite; a program needn't handle non-finite values.
Results may differ from a plain program's by a relative error of at most 0.0004.
Values sent between devices are 32-bit elements; how exact they have to be, the bound alone decides.
A program may use at most 128 MiB of HBM per device.

v0:
```python
import math

import jax
import jax.numpy as jnp
from jax import lax
from jax.sharding import PartitionSpec as P

ROUNDS = 2


def body(matrix, plan):
    rows_local = matrix.shape[0]
    width = matrix.shape[1]
    half_width = width // 2
    row_count = lax.axis_size("row")
    total_rows = rows_local * row_count
    col_count = width // row_count
    col_start = lax.axis_index("row") * col_count
    pair_index = lax.axis_index("pair")
    blocks_total = plan.shape[1]
    ramp_values = jnp.arange(width).astype(jnp.float32) / width
    identity_mat = jnp.eye(width, dtype=jnp.float32)
    identity_cols = lax.dynamic_slice_in_dim(identity_mat, col_start, col_count, 1)
    holders = jnp.arange(blocks_total)
    numbers = jnp.arange(blocks_total)
    pair_rows = matrix
    for round_index in range(ROUNDS):
        local_gram = lax.dot_general(
            pair_rows,
            pair_rows,
            (((0,), (0,)), ((), ())),
            precision=lax.Precision.HIGHEST,
            preferred_element_type=jnp.float32,
        )
        gram_sum = lax.psum(local_gram, "row")
        skew_part = gram_sum * (ramp_values[None, :] - ramp_values[:, None]) / math.sqrt(total_rows)
        skew_cols = lax.dynamic_slice_in_dim(skew_part, col_start, col_count, 1)
        square_slice = jnp.dot(
            skew_part,
            skew_cols,
            precision=lax.Precision.HIGHEST,
            preferred_element_type=jnp.float32,
        )
        square = lax.all_gather(square_slice, "row", axis=1, tiled=True)
        core_matrix = identity_mat - 0.25 * square
        lower_factor = jnp.linalg.cholesky(core_matrix)
        numer_cols = identity_cols + skew_cols + 0.25 * square_slice
        half_solved = lax.linalg.triangular_solve(
            lower_factor, numer_cols, left_side=True, lower=True
        )
        rotation_cols = lax.linalg.triangular_solve(
            lower_factor, half_solved, left_side=True, lower=True, transpose_a=True
        )

        def apply_rotation(piece, start, source=pair_rows):
            return jnp.dot(
                source, piece, precision=lax.Precision.HIGHEST, preferred_element_type=jnp.float32
            )

        turned = apply_rotation(
            lax.all_gather(rotation_cols, "row", axis=1, tiled=True), jnp.int32(0)
        )
        gathered = lax.all_gather(turned, "pair", axis=1, tiled=True)
        gathered = gathered.reshape(rows_local, blocks_total, half_width)
        targets = plan[round_index]
        wanted = lax.dynamic_slice_in_dim(targets, 2 * pair_index, 2, 0)
        matches = holders[None, :] == wanted[:, None]
        places = jnp.sum(jnp.where(matches, numbers[None, :], 0), axis=1)
        pair_rows = jnp.take(gathered, places, axis=1).reshape(rows_local, width)
        holders = targets
    return pair_rows


def solution(mesh):
    placed = (P("row", "pair"), P())
    return jax.shard_map(
        body, mesh=mesh, in_specs=placed, out_specs=P("row", "pair"), check_vma=False
    )
```

profile of v0, /device:TPU:1, one launch (start us, length us, event | category | flops | bytes accessed | tf_op | source)
XLA Modules:
  0.0 1565.8 jit_solution(12791502395133301801)
XLA Ops:
  15.4 195.7 %all-reduce.4.cloned.1.call-done = f32[1024,1024]{0,1:T(8,128)} async-done(((f32[1024,1024]{0,1:T(8,128)}), f32[1024,1024]{0,1:T(8,128)}) %all-reduce.4.cloned.1.call-update) | async-done | bytes 4194320 | tf_op jit(solution)/shard_map/psum | solution.py:35
  217.7 79.9 %all-gather.7.cloned.1.call-done = f32[1024,1024]{0,1:T(8,128)} async-done(((f32[1024,16]{0,1:T(8,128)}), f32[1024,1024]{0,1:T(8,128)}) %all-gather.7.cloned.1.call-update) | async-done | bytes 4194320 | tf_op jit(solution)/shard_map/all_gather | solution.py:44
  314.6 11.7 cholesky.619
  326.3 9.8 custom-call.59
  342.6 11.9 cholesky.638
  368.3 11.7 cholesky.659
  394.6 12.1 cholesky.678
  421.4 11.7 cholesky.697
  434.5 10.0 custom-call.63
  447.7 11.7 cholesky.716
  473.6 11.9 cholesky.735
  499.3 11.7 cholesky.752
  522.8 22.6 %while.8 = (s32[]{:T(128)}, f32[1024,1024]{1,0:T(8,128)}, s32[8,2]{0,1:T(2,128)S(1)}, f32[8,128,128]{2,1,0:T(8,128)S(1)}, s32[]{:T(128)}) while((s32[]{:T(128)}, f32[1024,1024]{1,0:T(8,128)}, s32[8,2]{0,1:T(2,128)S(1)}, f32[8,128,128]{2,1,0:T(8,128)S(1)}, s32[]{:T(128)}) %tuple.123), condition=%wide.while_cond.1, body=%wide.while_body.1.sunk | while | flops 2 | bytes 131181 | solution.py:51
  545.4 79.0 %custom-call.67 = f32[8,128,128]{1,2,0:T(8,128)S(1)} custom-call(f32[8,128,128]{2,1,0:T(8,128)S(1)} %get-tuple-element.38), custom_call_target="InvertDiagBlocksLowerTriangular" | custom-call | tf_op jit(solution)/shard_map/triangular_solve/custom-call.16 | solution.py:51
  646.1 76.4 %all-gather.9.cloned.1.call-done = f32[1024,1024]{0,1:T(8,128)} async-done(((f32[1024,16]{0,1:T(8,128)}), f32[1024,1024]{0,1:T(8,128)}) %all-gather.9.cloned.1.call-update) | async-done | bytes 4194320 | tf_op jit(solution)/shard_map/all_gather | solution.py:61
  729.5 47.4 %all-gather.11.cloned.1.call-done = f32[256,4096]{0,1:T(8,128)} async-done(((f32[256,1024]{0,1:T(8,128)}), f32[256,4096]{0,1:T(8,128)}) %all-gather.11.cloned.1.call-update) | async-done | bytes 4194320 | tf_op jit(solution)/shard_map/all_gather | solution.py:63
  785.0 194.4 %all-reduce.6.cloned.1.call-done = f32[1024,1024]{0,1:T(8,128)} async-done(((f32[1024,1024]{0,1:T(8,128)}), f32[1024,1024]{0,1:T(8,128)}) %all-reduce.6.cloned.1.call-update) | async-done | bytes 4194320 | tf_op jit(solution)/shard_map/psum | solution.py:35
  986.0 79.9 %all-gather.13.cloned.1.call-done = f32[1024,1024]{0,1:T(8,128)} async-done(((f32[1024,16]{0,1:T(8,128)}), f32[1024,1024]{0,1:T(8,128)}) %all-gather.13.cloned.1.call-update) | async-done | bytes 4194320 | tf_op jit(solution)/shard_map/all_gather | solution.py:44
  1082.8 11.7 cholesky.767
  1110.9 11.9 cholesky.786
  1137.8 11.7 cholesky.807
  1164.1 12.1 cholesky.826
  1190.8 11.7 cholesky.845
  1203.8 10.0 custom-call.72
  1217.1 11.7 cholesky.864
  1242.8 11.9 cholesky.883
  1268.5 11.7 cholesky.900
  1291.3 23.0 %while.9 = (s32[]{:T(128)}, f32[1024,1024]{1,0:T(8,128)}, s32[8,2]{0,1:T(2,128)S(1)}, f32[8,128,128]{2,1,0:T(8,128)S(1)}, s32[]{:T(128)}) while((s32[]{:T(128)}, f32[1024,1024]{1,0:T(8,128)}, s32[8,2]{0,1:T(2,128)S(1)}, f32[8,128,128]{2,1,0:T(8,128)S(1)}, s32[]{:T(128)}) %tuple.145), condition=%wide.while_cond.1.clone, body=%wide.while_body.1.clone.sunk | while | flops 2 | bytes 131181 | solution.py:51
  1314.3 78.8 %custom-call.76 = f32[8,128,128]{1,2,0:T(8,128)S(1)} custom-call(f32[8,128,128]{2,1,0:T(8,128)S(1)} %get-tuple-element.40), custom_call_target="InvertDiagBlocksLowerTriangular" | custom-call | tf_op jit(solution)/shard_map/triangular_solve/custom-call.16 | solution.py:51
  1414.9 76.4 %all-gather.15.cloned.1.call-done = f32[1024,1024]{0,1:T(8,128)} async-done(((f32[1024,16]{0,1:T(8,128)}), f32[1024,1024]{0,1:T(8,128)}) %all-gather.15.cloned.1.call-update) | async-done | bytes 4194320 | tf_op jit(solution)/shard_map/all_gather | solution.py:61
  1491.3 10.0 fusion.206
  1501.5 47.5 %all-gather.17.cloned.1.call-done = f32[256,4096]{1,0:T(8,128)} async-done(((f32[256,1024]{1,0:T(8,128)}), f32[256,4096]{1,0:T(8,128)}) %all-gather.17.cloned.1.call-update) | async-done | bytes 4194320 | tf_op jit(solution)/shard_map/all_gather | solution.py:63
  (306 shorter events, 356.7 us)
Async XLA Ops:
  6.5 1.2 copy-start
  6.5 204.6 %all-reduce.4.cloned.1.call-start = ((), (), s32[]{:S(2)}) async-start(), calls=%async_computation | async-start | bytes 8388608 | tf_op jit(solution)/shard_map/psum | solution.py:35
  12.8 284.7 %all-gather.7.cloned.1.call-start = ((), (), s32[]{:S(2)}) async-start(), calls=%async_computation.1 | async-start | bytes 4259840 | tf_op jit(solution)/shard_map/all_gather | solution.py:44
  217.6 504.9 %all-gather.9.cloned.1.call-start = ((), (), s32[]{:S(2)}) async-start(), calls=%async_computation.2 | async-start | bytes 4259840 | tf_op jit(solution)/shard_map/all_gather | solution.py:61
  312.6 2.0 copy-start.3
  643.4 85.8 %copy-start.6 = (s32[2,8]{1,0:T(2,128)S(1)}, s32[2,8]{1,0:T(2,128)}, u32[]{:S(2)}) copy-start(s32[2,8]{1,0:T(2,128)} %param.10) | copy-start | bytes 196
  645.4 0.6 copy-start.4
  646.1 130.9 %all-gather.11.cloned.1.call-start = ((), (), s32[]{:S(2)}) async-start(), calls=%async_computation.3 | async-start | bytes 5242880 | tf_op jit(solution)/shard_map/all_gather | solution.py:63
  729.1 250.2 %all-reduce.6.cloned.1.call-start = ((), (), s32[]{:S(2)}) async-start(), calls=%async_computation.4 | async-start | bytes 8388608 | tf_op jit(solution)/shard_map/psum | solution.py:35
  785.0 280.8 %all-gather.13.cloned.1.call-start = ((), (), s32[]{:S(2)}) async-start(), calls=%async_computation.5 | async-start | bytes 4259840 | tf_op jit(solution)/shard_map/all_gather | solution.py:44
  985.9 505.4 %all-gather.15.cloned.1.call-start = ((), (), s32[]{:S(2)}) async-start(), calls=%async_computation.6 | async-start | bytes 4259840 | tf_op jit(solution)/shard_map/all_gather | solution.py:61
  1080.9 1.9 copy-start.2
  1414.2 0.6 copy-start.5
  1414.8 134.2 %all-gather.17.cloned.1.call-start = ((), (), s32[]{:S(2)}) async-start(), calls=%async_computation.7 | async-start | bytes 5242880 | tf_op jit(solution)/shard_map/all_gather | solution.py:63
  1553.8 4.8 copy-start.1
Sparse Core Ops, SparseCore 0:
  13.0 198.0 all-reduce.3
  217.8 79.7 all-gather.6
  646.2 76.2 all-gather.8
  729.3 47.6 all-gather.10
  785.1 194.2 all-reduce.5
  986.0 79.7 all-gather.12
  1415.0 76.2 all-gather.14
  1501.4 47.5 all-gather.16
where the time goes:
time: 1570 us
  waiting for transfers between devices  798 us (51%)
  other arithmetic  541 us (34%)
  matrix products  121 us (8%)
  local copies, waits for them, and re-layouts  80.4 us (5%)
  between operations  24.9 us (2%)
    psum x2, waiting for transfers between devices, body(): gram_sum = lax.psum(local_gram, 'row')  390 us
    another operation x61, other arithmetic, body(): lower_factor = jnp.linalg.cholesky(core_matrix)  345 us
    another operation x5, other arithmetic, body(): lax.linalg.triangular_solve(lower_factor, half_solved, left_side=True, lo...  167 us
    all_gather x2, waiting for transfers between devices, body(): square = lax.all_gather(square_slice, 'row', axis=1, tiled=True)  160 us
    all_gather x2, waiting for transfers between devices, body(): lax.all_gather(rotation_cols, 'row', axis=1, tiled=True)  153 us
    all_gather x2, waiting for transfers between devices, body(): gathered = lax.all_gather(turned, 'pair', axis=1, tiled=True)  94.9 us
    another operation x28, matrix products, body(): lower_factor = jnp.linalg.cholesky(core_matrix)  46.2 us
    another operation x59, local copies, waits for them, and re-layouts, body(): lax.linalg.triangular_solve(lower_factor, half_solved, left_side=True, lo...  45.4 us
  transfers between devices with their start and end apart: 8, of which 8 were waited for; matrix products, arithmetic and copies ran while one was open for 0% of the time, Pallas kernels for 0%

commit v1 on v0

v1 whole, which is shorter than its diff:
```python
import functools

import jax
import jax.numpy as jnp
from jax import lax
from jax.experimental import pallas as pl
from jax.experimental.pallas import tpu as pltpu
from jax.sharding import PartitionSpec as P

ROUNDS = 2
F32 = jnp.float32
BF = jnp.bfloat16
MESH = pl.DeviceIdType.MESH
BLK = [(i, j) for i in range(8) for j in range(i, 8)]
NZ, NY = 8, 4
HALF, QUART, PIECE = 2304, 576, 72


def lb(x, c):
    return jnp.broadcast_to(x[:, c:c+1], (8,128))
def sb(x, s):
    return jnp.broadcast_to(x[s:s+1, :], (8,128))

def inv128(M, sub, lane, nb=16):
    M=list(M)
    for p in range(nb):
        R=[[lb(M[r],8*p+k) for k in range(8)] for r in [p]][0]
        E=list(R)
        inpan=(lane>=8*p)&(lane<8*p+8)
        for s in range(0,8,2):
            a=sb(E[s],s); b=sb(E[s+1],s); c=sb(E[s],s+1); d=sb(E[s+1],s+1)
            rd=1.0/(a*d-b*c)
            r0=sub==s; r1=sub==s+1
            ps,pq=E[s],E[s+1]
            new=list(E)
            for j in range(8):
                if j in (s,s+1): continue
                t0=sb(E[j],s); t1=sb(E[j],s+1)
                T0=(d*t0-b*t1)*rd
                T1=(a*t1-c*t0)*rd
                new[j]=jnp.where(r0,T0,jnp.where(r1,T1,E[j]-ps*T0-pq*T1))
            i00=d*rd; i01=-b*rd; i10=-c*rd; i11=a*rd
            new[s]=jnp.where(r0,i00,jnp.where(r1,i10,-(ps*i00+pq*i10)))
            new[s+1]=jnp.where(r0,i01,jnp.where(r1,i11,-(ps*i01+pq*i11)))
            E=new
        Mp=jnp.where(inpan,jnp.where(lane-8*p==sub,1.0,0.0),M[p])
        t=[E[k]*sb(Mp,k) for k in range(8)]
        N=((t[0]+t[1])+(t[2]+t[3]))+((t[4]+t[5])+(t[6]+t[7]))
        Nb=[sb(N,k) for k in range(8)]
        for r in range(nb):
            if r==p: continue
            base=jnp.where(inpan,0.0,M[r])
            t=[lb(M[r],8*p+k)*Nb[k] for k in range(8)]
            M[r]=base-(((t[0]+t[1])+(t[2]+t[3]))+((t[4]+t[5])+(t[6]+t[7])))
        M[p]=N
    return M

def split(x):
    hi=x.astype(BF); lo=(x-hi.astype(F32)).astype(BF)
    return hi,lo
def dot(a,b): return jnp.dot(a,b,preferred_element_type=F32)

def gram_kern(p_ref,g_ref,ph,plo,th,tl):
    for c in range(0,1024,256):
        x=p_ref[:,c:c+256]
        hi,lo=split(x)
        ph[:,c:c+256]=hi; plo[:,c:c+256]=lo
        xt=x.T
        hi,lo=split(xt)
        th[c:c+256,:]=hi; tl[c:c+256,:]=lo
    for bi in range(4):
        r=slice(256*bi,256*bi+256)
        for bj in range(bi,4):
            c=slice(256*bj,256*bj+256)
            g=dot(th[r,:],ph[:,c])+(dot(th[r,:],plo[:,c])+dot(tl[r,:],ph[:,c]))
            for u in range(2):
                for v in range(2):
                    ij=(2*bi+u,2*bj+v)
                    if ij in BLK:
                        n=BLK.index(ij)
                        g_ref[128*n:128*n+128,:]=g[128*u:128*u+128,128*v:128*v+128]

def gram(p):
    return pl.pallas_call(gram_kern,out_shape=jax.ShapeDtypeStruct((4608,128),F32),
      in_specs=[pl.BlockSpec(memory_space=pltpu.VMEM)],out_specs=pl.BlockSpec(memory_space=pltpu.VMEM),
      scratch_shapes=[pltpu.VMEM((256,1024),BF)]*2+[pltpu.VMEM((1024,256),BF)]*2,
      compiler_params=pltpu.CompilerParams(vmem_limit_bytes=60*2**20),name="gram")(p)

def solve_kern(parts,g_ref,p_ref,o_ref,c_ref,d_ref,dh_ref,dl_ref,ah_ref,al_ref):
    sub=lax.broadcasted_iota(jnp.int32,(8,128),0); lane=lax.broadcasted_iota(jnp.int32,(8,128),1)
    bi=lax.broadcasted_iota(jnp.int32,(128,128),0); bj=lax.broadcasted_iota(jnp.int32,(128,128),1)
    dif=(bj-bi).astype(F32)
    eye=jnp.where(bi==bj,1.0,0.0)
    for n,(i,j) in enumerate(BLK):
        k=g_ref[128*n:128*n+128,:]*((dif+128.0*(j-i))*(1.0/(1024*128*2)))
        if i==j:
            c_ref[128*i:128*i+128,128*i:128*i+128]=eye-k
        else:
            c_ref[128*i:128*i+128,128*j:128*j+128]=-k
            c_ref[128*j:128*j+128,128*i:128*i+128]=k.T
    c_ref[1024:1280,:]=p_ref[...]
    def step(k,_):
        k0=pl.multiple_of(k*128,128)
        kc=pl.ds(k0,128)
        if "inv" in parts:
            M=[c_ref[pl.ds(k0+8*r,8),kc] for r in range(16)]
            M=inv128(M,sub,lane)
            for r in range(16): d_ref[8*r:8*r+8,:]=M[r]
        c_ref[kc,kc]=jnp.zeros((128,128),F32)
        hi,lo=split(d_ref[...])
        dh_ref[...]=hi; dl_ref[...]=lo
        for c in range(0,1024,256):
            hi,lo=split(c_ref[kc,c:c+256])
            ah_ref[:,c:c+256]=hi; al_ref[:,c:c+256]=lo
        def rows(i,_):
            r=pl.ds(pl.multiple_of(i*128,128),128)
            xh,xl=split(c_ref[r,kc])
            y=dot(xh,dh_ref[...])+(dot(xh,dl_ref[...])+dot(xl,dh_ref[...]))
            yh,yl=split(y)
            for c in range(0,1024,256):
                cs=slice(c,c+256)
                c_ref[r,cs]=c_ref[r,cs]-(dot(yh,ah_ref[:,cs])+(dot(yh,al_ref[:,cs])+dot(yl,ah_ref[:,cs])))
            c_ref[r,kc]=y
            return 0
        if "upd" in parts:
            lax.fori_loop(k+1,10,rows,0)
        return 0
    lax.fori_loop(0,8,step,0)
    o_ref[...]=2.0*c_ref[1024:1280,:]-p_ref[...]

def solve(g,p,parts=("inv","upd")):
    import functools
    return pl.pallas_call(functools.partial(solve_kern,parts),out_shape=jax.ShapeDtypeStruct((256,1024),F32),
      in_specs=[pl.BlockSpec(memory_space=pltpu.VMEM)]*2,out_specs=pl.BlockSpec(memory_space=pltpu.VMEM),
      scratch_shapes=[pltpu.VMEM((1280,1024),F32),pltpu.VMEM((128,128),F32),pltpu.VMEM((128,128),BF),pltpu.VMEM((128,128),BF),pltpu.VMEM((128,1024),BF),pltpu.VMEM((128,1024),BF)],
      compiler_params=pltpu.CompilerParams(vmem_limit_bytes=60*2**20),name="solve")(g,p)

def comm_kern(g_ref,o_ref,r1,r2,r3,h,q,s1,v1,s2,v2,s3,v3,s4,v4,s5,v5,s6,v6):
    row=lax.axis_index("row")
    c=lax.rem(row,2); y=lax.rem(row//2,NY); z=row//(2*NY)
    def dev(zz,yy,cc): return {"row":(zz*NY+yy)*2+cc}
    other=dev(z,y,1-c)
    ys=[lax.rem(y+d,NY) for d in range(NY)]
    zs=[lax.rem(z+d,NZ) for d in range(NZ)]
    ydev=[dev(z,ys[d],c) for d in range(NY)]
    zdev=[dev(zs[d],y,c) for d in range(NZ)]
    bar=pltpu.get_barrier_semaphore()
    for t in [other]+ydev[1:]+zdev[1:]:
        pl.semaphore_signal(bar,inc=1,device_id=t,device_id_type=MESH)
    pl.semaphore_wait(bar,1+(NY-1)+(NZ-1))
    def rc(src,dst,ss,rs,t):
        return pltpu.make_async_remote_copy(src_ref=src,dst_ref=dst,send_sem=ss,recv_sem=rs,device_id=t,device_id_type=MESH)
    order=[1,3,2,0]
    c1=[]
    for d in order:
        yo=pl.multiple_of(ys[d]*QUART,8)
        cp=rc(g_ref.at[pl.ds(pl.multiple_of((1-c)*HALF+yo,8),QUART)],r1.at[pl.ds(yo,QUART)],s1.at[d],v1.at[d],other)
        cp.start(); c1.append(cp)
    c2=[]
    for n,d in enumerate(order):
        yo=pl.multiple_of(ys[d]*QUART,8)
        c1[n].wait_recv()
        h[pl.ds(yo,QUART),:]=g_ref[pl.ds(pl.multiple_of(c*HALF+yo,8),QUART),:]+r1[pl.ds(yo,QUART),:]
        if d:
            cp=rc(h.at[pl.ds(yo,QUART)],r2.at[d-1],s2.at[d-1],v2.at[d-1],ydev[d])
            cp.start(); c2.append(cp)
    for cp in c2: cp.wait_recv()
    c3=[]
    yo=pl.multiple_of(y*QUART,8)
    for d in [4,3,5,2,6,1,7,0]:
        zo=pl.multiple_of(zs[d]*PIECE,8)
        zr=pl.ds(zo,PIECE)
        q[zr,:]=(h[pl.ds(pl.multiple_of(yo+zo,8),PIECE),:]+r2[0,zr,:])+(r2[1,zr,:]+r2[2,zr,:])
        if d:
            cp=rc(q.at[zr],r3.at[d-1],s3.at[d-1],v3.at[d-1],zdev[d])
            cp.start(); c3.append(cp)
    zr=pl.ds(pl.multiple_of(z*PIECE,8),PIECE)
    for cp in c3: cp.wait_recv()
    t=q[zr,:]
    for d in range(NZ-1): t=t+r3[d]
    mine=pl.ds(pl.multiple_of(c*HALF+yo+z*PIECE,8),PIECE)
    o_ref[mine,:]=t
    c4=[]
    for d in [4,3,5,2,6,1,7]:
        cp=rc(o_ref.at[mine],o_ref.at[mine],s4.at[d-1],v4.at[d-1],zdev[d])
        cp.start(); c4.append(cp)
    for cp in c4: cp.wait_recv()
    quarter=pl.ds(pl.multiple_of(c*HALF+yo,8),QUART)
    c5=[];c6=[]
    for d in [1,3,2]:
        cp=rc(o_ref.at[quarter],o_ref.at[quarter],s5.at[d-1],v5.at[d-1],ydev[d])
        cp.start(); c5.append(cp)
    cp=rc(o_ref.at[quarter],o_ref.at[quarter],s6.at[0],v6.at[0],other)
    cp.start(); c6.append(cp)
    for n,d in enumerate([1,3,2]):
        c5[n].wait_recv()
        src=pl.ds(pl.multiple_of(c*HALF+lax.rem(y+NY-d,NY)*QUART,8),QUART)
        cp=rc(o_ref.at[src],o_ref.at[src],s6.at[d],v6.at[d],other)
        cp.start(); c6.append(cp)
    for cp in c6: cp.wait_recv()
    for cp in c1+c2+c3+c4+c5+c6: cp.wait_send()

def comm(g):
    D=pltpu.SemaphoreType.DMA
    return pl.pallas_call(comm_kern,out_shape=jax.ShapeDtypeStruct((4608,128),F32),
      in_specs=[pl.BlockSpec(memory_space=pltpu.VMEM)],out_specs=pl.BlockSpec(memory_space=pltpu.VMEM),
      scratch_shapes=[pltpu.VMEM((HALF,128),F32),pltpu.VMEM((3,QUART,128),F32),pltpu.VMEM((7,PIECE,128),F32),pltpu.VMEM((HALF,128),F32),pltpu.VMEM((QUART,128),F32)]
        +[D((4,)),D((4,)),D((3,)),D((3,)),D((7,)),D((7,)),D((7,)),D((7,)),D((3,)),D((3,)),D((4,)),D((4,))],
      compiler_params=pltpu.CompilerParams(vmem_limit_bytes=60*2**20,collective_id=0,has_side_effects=True),name="comm")(g)

def body(matrix, plan):
    rows_local, width = matrix.shape
    half_width = width // 2
    pair_index = lax.axis_index("pair")
    blocks_total = plan.shape[1]
    holders = jnp.arange(blocks_total)
    numbers = jnp.arange(blocks_total)
    pair_rows = matrix
    for round_index in range(ROUNDS):
        turned = solve(comm(gram(pair_rows)), pair_rows)
        gathered = lax.all_gather(turned, "pair", axis=1, tiled=True)
        gathered = gathered.reshape(rows_local, blocks_total, half_width)
        targets = plan[round_index]
        wanted = lax.dynamic_slice_in_dim(targets, 2 * pair_index, 2, 0)
        matches = holders[None, :] == wanted[:, None]
        places = jnp.sum(jnp.where(matches, numbers[None, :], 0), axis=1)
        pair_rows = jnp.take(gathered, places, axis=1).reshape(rows_local, width)
        holders = targets
    return pair_rows


def solution(mesh):
    placed = (P("row", "pair"), P())
    return jax.shard_map(
        body, mesh=mesh, in_specs=placed, out_specs=P("row", "pair"), check_vma=False
    )
```

time: 1570 us -> 382 us (0.24)
  waiting for transfers between devices: 798 us -> 92.7 us
  other arithmetic: 541 us -> 0.81 us
  Pallas kernels: 0 us -> 256 us
  matrix products: 121 us -> 0 us
  local copies, waits for them, and re-layouts: 80.4 us -> 18 us
    another operation x66 -> x0, other arithmetic: 513 us -> none  [the longest x61 345 us: body(): lower_factor = jnp.linalg.cholesky(core_matrix)]
    psum x2 -> x0, waiting for transfers between devices: 390 us -> none  [body(): gram_sum = lax.psum(local_gram, 'row')]
    all_gather x4 -> x0, waiting for transfers between devices: 313 us -> none  [the longest x2 160 us: body(): square = lax.all_gather(square_slice, 'row', axis=1, tiled=True)]
    pallas_call x0 -> x6, Pallas kernels: none -> 256 us  [the longest x2 125 us: solve(): pl.pallas_call(functools.partial(solve_kern, parts), out_shape=jax.ShapeD...]
    another operation x88 -> x0, matrix products: 87.3 us -> none  [the longest x28 46.2 us: body(): lower_factor = jnp.linalg.cholesky(core_matrix)]
    another operation x75 -> x0, local copies, waits for them, and re-layouts: 50.5 us -> none  [the longest x59 45.4 us: body(): lax.linalg.triangular_solve(lower_factor, half_solved, left_side=True, lo...]
    dot_general x6 -> x0, matrix products: 34.2 us -> none  [the longest x2 16.6 us: apply_rotation(): jnp.dot(source, piece, precision=lax.Precision.HIGHEST, preferred_element...]
  transfers between devices with their start and end apart: 8 -> 2, of which waited for: 8 -> 2; matrix products, arithmetic and copies ran while one was open for 0% -> 0% of each run, Pallas kernels for 0% -> 0%
where the time goes in v1:
time: 382 us; the launch traced here: 381 us
  Pallas kernels  256 us (67%)
  waiting for transfers between devices  92.7 us (24%)
  local copies, waits for them, and re-layouts  18 us (5%)
  between operations  13.5 us (4%)
    pallas_call x2, Pallas kernels, solve(): pl.pallas_call(functools.partial(solve_kern, parts), out_shape=jax.ShapeD...  125 us
    pallas_call x2, Pallas kernels, comm(): pl.pallas_call(comm_kern, out_shape=jax.ShapeDtypeStruct((4608, 128), F32...  123 us
    all_gather x2, waiting for transfers between devices, body(): gathered = lax.all_gather(turned, 'pair', axis=1, tiled=True)  92.6 us
    reshape x2, local copies, waits for them, and re-layouts, body(): gathered = gathered.reshape(rows_local, blocks_total, half_width)  9.57 us
    pallas_call x2, Pallas kernels, gram(): pl.pallas_call(gram_kern, out_shape=jax.ShapeDtypeStruct((4608, 128), F32...  7.74 us
  transfers between devices with their start and end apart: 2, of which 2 were waited for; matrix products, arithmetic and copies ran while one was open for 0% of the time, Pallas kernels for 0%

profile of v1, /device:TPU:1, one launch (start us, length us, event | category | flops | bytes accessed | tf_op | source)
XLA Modules:
  0.0 381.2 jit_solution(16343292133731417299)
XLA Ops:
  6.5 0.0 all-gather.3.cloned.1.call-start
  6.5 3.9 %gram.2.g_ref = f32[4608,128]{1,0:T(8,128)} custom-call(f32[256,1024]{1,0:T(8,128)} %p_ref.3), custom_call_target="tpu_custom_call" | custom-call | tf_op jit(solution)/shard_map/gram/pallas_call | solution.py:84
  10.4 0.0 copy-start
  10.4 63.0 %comm.2.g_ref = f32[4608,128]{1,0:T(8,128)} custom-call(f32[4608,128]{1,0:T(8,128)} %gram.2.g_ref), custom_call_target="tpu_custom_call" | custom-call | tf_op jit(solution)/shard_map/comm/pallas_call | solution.py:205
  73.4 62.5 %solve.2 = f32[256,1024]{1,0:T(8,128)} custom-call(f32[4608,128]{1,0:T(8,128)} %comm.2.g_ref, f32[256,1024]{1,0:T(8,128)} %p_ref.3), custom_call_target="tpu_custom_call" | custom-call | tf_op jit(solution)/shard_map/solve/pallas_call | solution.py:133
  135.9 0.0 all-gather.3.cloned.1.call-update
  135.9 0.2 all-gather.5.cloned.1.call-start
  136.1 0.0 copy-done
  136.2 0.1 dynamic-slice_bitcast_fusion
  136.2 0.2 fusion
  136.5 46.2 %all-gather.3.cloned.1.call-done = f32[256,4096]{1,0:T(8,128)} async-done(((f32[256,1024]{1,0:T(8,128)}), f32[256,4096]{1,0:T(8,128)}) %all-gather.3.cloned.1.call-update) | async-done | bytes 4194320 | tf_op jit(solution)/shard_map/all_gather | solution.py:221
  182.7 4.8 %copy.22 = f32[32,8,8,512]{3,2,0,1:T(8,128)} copy(f32[32,8,8,512]{3,2,1,0:T(8,128)} %bitcast.25) | data formatting | bytes 8388608 | tf_op jit(solution)/shard_map/reshape | solution.py:222
  187.5 2.8 gather_fusion
  190.3 0.2 select_bitcast_fusion.1
  190.5 1.1 copy.18
  191.6 3.9 %gram.3.g_ref = f32[4608,128]{1,0:T(8,128)} custom-call(f32[256,1024]{1,0:T(8,128)} %bitcast.21), custom_call_target="tpu_custom_call" | custom-call | tf_op jit(solution)/shard_map/gram/pallas_call | solution.py:84
  195.4 60.4 %comm.3.g_ref = f32[4608,128]{1,0:T(8,128)} custom-call(f32[4608,128]{1,0:T(8,128)} %gram.3.g_ref), custom_call_target="tpu_custom_call" | custom-call | tf_op jit(solution)/shard_map/comm/pallas_call | solution.py:205
  255.9 62.5 %solve.3 = f32[256,1024]{1,0:T(8,128)} custom-call(f32[4608,128]{1,0:T(8,128)} %comm.3.g_ref, f32[256,1024]{1,0:T(8,128)} %bitcast.22), custom_call_target="tpu_custom_call" | custom-call | tf_op jit(solution)/shard_map/solve/pallas_call | solution.py:133
  318.3 0.0 all-gather.5.cloned.1.call-update
  318.4 0.2 fusion.1
  318.6 46.4 %all-gather.5.cloned.1.call-done = f32[256,4096]{1,0:T(8,128)} async-done(((f32[256,1024]{1,0:T(8,128)}), f32[256,4096]{1,0:T(8,128)}) %all-gather.5.cloned.1.call-update) | async-done | bytes 4194320 | tf_op jit(solution)/shard_map/all_gather | solution.py:221
  365.0 4.8 %copy.21 = f32[32,8,8,512]{3,2,0,1:T(8,128)} copy(f32[32,8,8,512]{3,2,1,0:T(8,128)} %bitcast.26) | data formatting | bytes 8388608 | tf_op jit(solution)/shard_map/reshape | solution.py:222
  369.7 2.8 gather_fusion.1
  372.5 0.2 select_bitcast_fusion
  372.8 0.3 copy.14
  373.1 1.3 copy.15
  (7 shorter events, 0.1 us)
Async XLA Ops:
  6.5 176.2 %all-gather.3.cloned.1.call-start = ((), (), s32[]{:S(2)}) async-start(), calls=%async_computation | async-start | bytes 5242880 | tf_op jit(solution)/shard_map/all_gather | solution.py:221
  10.4 125.7 %copy-start = (s32[2,8]{1,0:T(2,128)S(1)}, s32[2,8]{1,0:T(2,128)}, u32[]{:S(2)}) copy-start(s32[2,8]{1,0:T(2,128)} %param.5) | copy-start | bytes 196
  135.9 229.1 %all-gather.5.cloned.1.call-start = ((), (), s32[]{:S(2)}) async-start(), calls=%async_computation.1 | async-start | bytes 5242880 | tf_op jit(solution)/shard_map/all_gather | solution.py:221
Sparse Core Ops, SparseCore 0:
  136.0 46.6 all-gather.2
  318.5 46.4 all-gather.4
